TPU v7x, 256 devices: a whole 4x4x8 slice. The times are simulated.
256 devices in a mesh: dp: 4 (over x), ctx: 16 (over z, core), exp: 4 (over y).
Axes of the slice: x: 4, y: 4, z: 8, core: 2. Of those that a mesh axis runs over, the one named last changes fastest.
Arguments:
- d_out: bfloat16 [4, 8192, 5120], P('dp', ('ctx', 'exp')), may hold values from -3 to 3
- route_ids: int32 [4, 8192, 6], P('dp', ('ctx', 'exp')), may hold values from 0 to 63, all different within a row; in each aligned block of 128 rows (0 to 127, 128 to 255, ..., all dimensions but the last counted through in order) at most 14 rows name the same one
- gate_weights: float32 [4, 8192, 6], P('dp', ('ctx', 'exp')), may hold values from 0.1 to 2
- saved_hidden: bfloat16 [4, 64, 896, 768], P('dp', ('ctx', 'exp')), may hold values from -6 to 6
- down_weight: bfloat16 [64, 5120, 768], P(('ctx', 'exp'), 'dp'), may hold values from -0.21875 to 0.21875
Outputs:
- d_hidden: bfloat16 [4, 64, 896, 768], P('dp', ('ctx', 'exp'))
- weight_grad: float32 [64, 5120, 768], P(('ctx', 'exp'), 'dp')
Inputs may be any that keep to these rules, and one draw needn't show every extreme that they name: `route_ids`: each token names 6 different experts; within a sequence the tokens of one device (aligned blocks of 128) name no expert more than 14 times, and some block names one exactly 14 times.
All inputs are finite; a program needn't handle non-finite values.
Results may differ from a plain program's by a relative error of at most 0.0049.
Values may be sent and summed in bfloat16 or wider, within the bound.
A program may use at most 128 MiB of HBM per device.

v0:
```python
import jax
import jax.numpy as jnp
from jax import lax
from jax.sharding import PartitionSpec as P


def body(d_out, route_ids, gate_weights, saved_hidden, down_weight):
    ctx_count = lax.axis_size("ctx")
    exp_count = lax.axis_size("exp")
    expert_count = ctx_count * exp_count
    model_width = d_out.shape[2]
    capacity = saved_hidden.shape[2] // expert_count
    flat_ids = route_ids[0].reshape(-1)
    onehot = (flat_ids[:, None] == jnp.arange(expert_count, dtype=jnp.int32)[None, :]).astype(
        jnp.int32
    )
    before = jnp.cumsum(onehot, axis=0) - onehot
    position = jnp.sum(before * onehot, axis=1)
    target = flat_ids * capacity + position
    slot_rows = (
        (gate_weights[0][:, :, None] * d_out[0][:, None, :].astype(jnp.float32))
        .astype(jnp.bfloat16)
        .reshape(-1, model_width)
    )
    outgoing = (
        jnp.zeros((expert_count * capacity, model_width), jnp.bfloat16).at[target].set(slot_rows)
    )
    by_peer = outgoing.reshape(expert_count, capacity, model_width)
    arrived = lax.all_to_all(by_peer, ("ctx", "exp"), split_axis=0, concat_axis=0, tiled=True)
    routed = arrived.reshape(expert_count * capacity, model_width)
    hidden = saved_hidden[0, 0]
    columns = routed
    d_rows = jnp.dot(
        columns,
        lax.all_gather(down_weight, "dp", axis=1, tiled=True)[0],
        preferred_element_type=jnp.float32,
    )
    columns = routed
    weight_shard = lax.psum_scatter(
        lax.dot_general(
            columns, hidden, (((0,), (0,)), ((), ())), preferred_element_type=jnp.float32
        ),
        "dp",
        scatter_dimension=0,
        tiled=True,
    )
    return (d_rows.astype(jnp.bfloat16)[None, None], weight_shard[None])


def solution(mesh):
    return jax.shard_map(
        body,
        mesh=mesh,
        in_specs=(
            P("dp", ("ctx", "exp"), None),
            P("dp", ("ctx", "exp"), None),
            P("dp", ("ctx", "exp"), None),
            P("dp", ("ctx", "exp"), None, None),
            P(("ctx", "exp"), "dp", None),
        ),
        out_specs=(P("dp", ("ctx", "exp"), None, None), P(("ctx", "exp"), "dp", None)),
        check_vma=False,
    )
```

profile of v0, /device:TPU:6, one launch (start us, length us, event | category | flops | bytes accessed | tf_op | source)
XLA Modules:
  0.0 499.7 jit_solution(5612280568122559249)
XLA Ops:
  7.2 0.0 copy-start
  7.2 0.9 copy.8
  8.1 0.1 eq.29
  8.2 0.1 eq.25
  8.4 0.7 broadcast_multiply_fusion
  9.1 1.8 reduce-window.6
  10.9 0.3 slice_reduce_fusion
  11.2 0.1 copy.7
  11.3 0.1 mul.39
  11.4 1.6 bitcast_convert_fusion
  13.0 7.6 %mul.43 = f32[128,6,5120]{2,1,0:T(8,128)} broadcast(f32[128,5120]{1,0:T(8,128)S(1)} %bitcast_convert_fusion), dimensions={0,2} | broadcast | bytes 18350080 | tf_op jit(solution)/shard_map/mul | solution.py:21
  20.6 0.0 copy-start.2
  20.6 18.4 %mul.44 = f32[768,5120]{1,0:T(8,128)} reshape(f32[128,6,5120]{2,1,0:T(8,128)} %mul.43) | data formatting | bytes 31457280 | tf_op jit(solution)/shard_map/mul | solution.py:21
  39.0 0.0 copy-done.2
  39.0 0.1 copy.11
  39.1 0.1 mul.41
  39.3 0.1 fusion.14
  39.4 8.8 %multiply_convert_fusion = bf16[768,5120]{1,0:T(8,128)(2,1)} fusion(f32[768,5120]{1,0:T(8,128)} %mul.44, f32[768]{0:T(1024)S(1)} %mul.41), kind=kLoop, calls=%fused_computation.1 | loop fusion | flops 7864320 | bytes 23596032 | tf_op jit(solution)/shard_map/convert_element_type | solution.py:22
  48.2 21.0 %scatter_custom_fusion = bf16[896,5120]{1,0:T(8,128)(2,1)} fusion(s32[768]{0:T(1024)S(1)} %fusion.16, bf16[768,5120]{1,0:T(8,128)(2,1)} %multiply_convert_fusion, bf16[]{:T(256)} %constant.4.clone.1), kind=kCustom, calls=%fused_computation.4 | custom fusion | bytes 9175552 | tf_op jit(solution)/shard_map/scatter | solution.py:26
  69.2 13.5 %reshape.70 = bf16[64,14,5120]{2,1,0:T(8,128)(2,1)} reshape(bf16[896,5120]{1,0:T(8,128)(2,1)} %scatter_custom_fusion) | data formatting | bytes 18350080 | tf_op jit(solution)/shard_map/reshape | solution.py:28
  82.7 12.3 %all-to-all-start = ((bf16[64,14,5120]{2,1,0:T(8,128)(2,1)}), bf16[64,14,5120]{2,1,0:T(8,128)(2,1)}, u32[]{:S(2)}, u32[]{:S(2)}) async-start(bf16[64,14,5120]{2,1,0:T(8,128)(2,1)} %reshape.70), calls=%async_computation | async-start | bytes 20971520 | tf_op jit(solution)/shard_map/all_to_all | solution.py:29
  95.0 0.0 all-gather.2.cloned.1.call-start
  95.1 0.7 all-gather.2.cloned.1.call-update
  95.7 0.0 reduce-scatter.2.cloned.1.call-start
  95.8 226.8 %all-to-all-done = bf16[64,14,5120]{2,1,0:T(8,128)(2,1)} async-done(((bf16[64,14,5120]{2,1,0:T(8,128)(2,1)}), bf16[64,14,5120]{2,1,0:T(8,128)(2,1)}, u32[]{:S(2)}, u32[]{:S(2)}) %all-to-all-start) | async-done | bytes 9175072 | tf_op jit(solution)/shard_map/all_to_all | solution.py:29
  322.6 13.6 %reshape.71 = bf16[896,5120]{1,0:T(8,128)(2,1)} reshape(bf16[64,14,5120]{2,1,0:T(8,128)(2,1)} %all-to-all-done) | data formatting | bytes 18350080 | tf_op jit(solution)/shard_map/reshape | solution.py:30
  336.2 0.0 copy-done
  336.2 14.8 %fusion.10 = f32[5120,768]{1,0:T(8,128)} fusion(bf16[896,5120]{1,0:T(8,128)(2,1)} %reshape.71, bf16[1,1,896,768]{3,2,1,0:T(8,128)(2,1)S(1)} %copy-done), kind=kOutput, calls=%fused_computation.8 | convolution fusion | flops 7046430720 | bytes 26279936 | tf_op jit(solution)/shard_map/dot_general | solution.py:40
  351.0 0.0 reduce-scatter.2.cloned.1.call-update
  351.0 0.0 all-gather.2.cloned.1.call-done
  351.1 0.0 copy-start.1
  351.1 13.0 %fusion.7 = bf16[1,1,896,768]{3,2,1,0:T(8,128)(2,1)} fusion(bf16[896,5120]{1,0:T(8,128)(2,1)} %reshape.71, bf16[1,5120,768]{2,1,0:T(8,128)(2,1)} %all-gather.2.cloned.1.call-done), kind=kOutput, calls=%fused_computation.7 | convolution fusion | flops 7047118848 | bytes 18415616 | tf_op jit(solution)/shard_map/dot_general | solution.py:33
  364.1 128.7 %reduce-scatter.2.cloned.1.call-done = f32[1280,768]{1,0:T(8,128)} async-done(((f32[5120,768]{1,0:T(8,128)}), f32[1280,768]{1,0:T(8,128)}) %reduce-scatter.2.cloned.1.call-update) | async-done | bytes 3932176 | tf_op jit(solution)/shard_map/reduce_scatter | solution.py:39
  492.8 0.0 copy-done.1
  (3 shorter events, 0.1 us)
Async XLA Ops:
  7.2 329.0 %copy-start = (bf16[1,1,896,768]{3,2,1,0:T(8,128)(2,1)S(1)}, bf16[1,1,896,768]{3,2,1,0:T(8,128)(2,1)}, u32[]{:S(2)}) copy-start(bf16[1,1,896,768]{3,2,1,0:T(8,128)(2,1)} %param.8) | copy-start | bytes 4128772
  20.6 18.4 %copy-start.2 = (f32[1,128,6]{1,0,2:T(1,128)S(1)}, f32[1,128,6]{1,0,2:T(1,128)}, u32[]{:S(2)}) copy-start(f32[1,128,6]{1,0,2:T(1,128)} %param.7) | copy-start | bytes 9220
  82.7 239.9 %all-to-all-start = ((bf16[64,14,5120]{2,1,0:T(8,128)(2,1)}), bf16[64,14,5120]{2,1,0:T(8,128)(2,1)}, u32[]{:S(2)}, u32[]{:S(2)}) async-start(bf16[64,14,5120]{2,1,0:T(8,128)(2,1)} %reshape.70), calls=%async_computation | async-start | bytes 20971520 | tf_op jit(solution)/shard_map/all_to_all | solution.py:29
  95.0 256.0 %all-gather.2.cloned.1.call-start = ((), (), s32[]{:S(2)}) async-start(), calls=%async_computation.2 | async-start | bytes 9830400 | tf_op jit(solution)/shard_map/all_gather | solution.py:35
  95.7 397.1 %reduce-scatter.2.cloned.1.call-start = ((), (), s32[]{:S(2)}) async-start(), calls=%async_computation.3 | async-start | bytes 19660800 | tf_op jit(solution)/shard_map/reduce_scatter | solution.py:39
  351.1 141.8 %copy-start.1 = (bf16[1,1,896,768]{3,2,1,0:T(8,128)(2,1)S(1)}, bf16[1,1,896,768]{3,2,1,0:T(8,128)(2,1)}, u32[]{:S(2)}) copy-start(bf16[1,1,896,768]{3,2,1,0:T(8,128)(2,1)} %param.8) | copy-start | bytes 4128772
Sparse Core Ops, SparseCore 0:
  97.7 81.0 all-gather.1
  351.2 141.6 reduce-scatter.1
where the time goes:
time: 504 us; the launch traced here: 500 us
  waiting for transfers between devices  356 us (71%)
  local copies, waits for them, and re-layouts  76 us (15%)
  matrix products  27.8 us (6%)
  between operations  14.1 us (3%)
  other arithmetic  13 us (3%)
  starting transfers between devices  12.4 us (2%)
    all_to_all x1, waiting for transfers between devices, body(): lax.all_to_all(by_peer, ('ctx', 'exp'), split_axis=0, concat_axis=0, tile...  227 us
    reduce_scatter x1, waiting for transfers between devices, body(): lax.psum_scatter(lax.dot_general(columns, hidden, (((0,), (0,)), ((), ())...  129 us
    mul x3, local copies, waits for them, and re-layouts, body(): gate_weights[0][:, :, None] * d_out[0][:, None, :].astype(jnp.float32)  26.1 us
    scatter x1, local copies, waits for them, and re-layouts, body(): jnp.zeros((expert_count * capacity, model_width), jnp.bfloat16).at[target]  21 us
    dot_general x1, matrix products, body(): lax.dot_general(columns, hidden, (((0,), (0,)), ((), ())), preferred_elem...  14.8 us
    reshape x1, local copies, waits for them, and re-layouts, body(): routed = arrived.reshape(expert_count * capacity, model_width)  13.6 us
    reshape x1, local copies, waits for them, and re-layouts, body(): by_peer = outgoing.reshape(expert_count, capacity, model_width)  13.5 us
    dot_general x1, matrix products, body(): jnp.dot(columns, lax.all_gather(down_weight, 'dp', axis=1, tiled=True)[0]...  13 us
  transfers between devices with their start and end apart: 3, of which 2 were waited for; matrix products, arithmetic and copies ran while one was open for 8% of the time, Pallas kernels for 0%

commit v1 on v0

v1 whole, which is shorter than its diff:
```python
import functools

import jax
import jax.numpy as jnp
from jax import lax
from jax.experimental import pallas as pl
from jax.experimental.pallas import tpu as pltpu
from jax.sharding import PartitionSpec as P

MESH = pl.DeviceIdType.MESH
F32, BF16, I32 = jnp.float32, jnp.bfloat16, jnp.int32

NX, NY, NZ, NC = 4, 4, 8, 2
TOK, CAP, FF = 128, 14, 768
GROUPS = NY * NC
PART = NZ * CAP
SLOTS = GROUPS * PART
WIDTH = 1280
HALF = SLOTS // 2
TILE = 128

CHUNKS = (
    (0, 0, 256),
    (2, 0, 640),
    (2, 640, 640),
    (1, 0, 640),
    (1, 640, 640),
    (3, 0, 640),
    (3, 640, 640),
    (0, 256, 512),
    (0, 768, 512),
)
NK = len(CHUNKS)
COL = [sum(c[2] for c in CHUNKS[:k]) for k in range(NK)]
WMAX = max(c[2] for c in CHUNKS)
NSB = 3
HOPS = [(4, 3) if k % 2 == 0 else (3, 4) for k in range(NK)]


def kernel(
    d_out, ids_t, gate_t, hidden, weight, dh_out, wg_out,
    rows, sendbuf, routed, hid, raw, wts, acc, part, part2, partr,
    meta, plane, target,
    loc_sem, xs, xr, ms, mr, gs, gr, rs, rr, ys, yr, hs, hr, ps, pr,
):
    i = lax.axis_index("dp")
    ctx = lax.axis_index("ctx")
    y = lax.axis_index("exp")
    z = ctx // NC
    c = lax.rem(ctx, NC)

    def dev(dx=0, dz=0, dc=0, dy=0):
        return (
            lax.rem(i + dx, NX),
            lax.rem(z + dz, NZ) * NC + lax.rem(c + dc, NC),
            lax.rem(y + dy, NY),
        )

    def remote(src, dst, send, recv, to):
        return pltpu.make_async_remote_copy(
            src_ref=src, dst_ref=dst, send_sem=send, recv_sem=recv, device_id=to, device_id_type=MESH
        )

    load_hidden = pltpu.make_async_copy(hidden.at[0, 0], raw, loc_sem.at[0])
    load_hidden.start()
    load_weight = pltpu.make_async_copy(weight.at[0], wts, loc_sem.at[1])
    load_weight.start()
    own = {}
    for k, (o, first, w) in enumerate(CHUNKS):
        if o == 0:
            start = pl.multiple_of(i * WIDTH + first, 128)
            own[k] = pltpu.make_async_copy(
                d_out.at[0, :, pl.ds(start, w)], rows.at[0:TOK, COL[k] : COL[k] + w], loc_sem.at[2 + k]
            )
            own[k].start()

    barrier = pltpu.get_barrier_semaphore()
    peers = [dict(dx=a) for a in range(1, NX)] + [dict(dz=a) for a in range(1, NZ)]
    peers += [dict(dc=j // NY, dy=j % NY) for j in range(1, GROUPS)]
    for p in peers:
        pl.semaphore_signal(barrier, inc=1, device_id=dev(**p), device_id_type=MESH)

    r = lax.broadcasted_iota(I32, (NZ * GROUPS, TOK), 0)
    dz, dc, dy = r // GROUPS, (r // NY) % NC, r % NY
    expert = ((z + dz) % NZ) * GROUPS + ((c + dc) % NC) * NY + (y + dy) % NY
    gates = jnp.zeros((NZ * GROUPS, TOK), F32)
    for k in range(ids_t.shape[0]):
        gates += jnp.where(ids_t[k : k + 1, :] == expert, gate_t[k : k + 1, :], 0.0)
    meta[0] = gates.reshape(NZ, GROUPS, TOK)

    pl.semaphore_wait(barrier, len(peers))

    mcopy = {}
    for o in range(1, NX):
        mcopy[o] = remote(meta.at[0], meta.at[o], ms.at[o], mr.at[o], dev(dx=NX - o))
        mcopy[o].start()
    xcopy = {}
    for k, (o, first, w) in enumerate(CHUNKS):
        if o:
            start = pl.multiple_of(lax.rem(i + NX - o, NX) * WIDTH + first, 128)
            xcopy[k] = remote(
                d_out.at[0, :, pl.ds(start, w)], rows.at[0:TOK, COL[k] : COL[k] + w],
                xs.at[k], xr.at[k], dev(dx=NX - o),
            )
            xcopy[k].start()

    ring_copies = []

    def ring_copy(k, way, hop):
        lo, hi = COL[k], COL[k] + CHUNKS[k][2]
        if way == 0:
            src, dst, to = (NZ + 1 - hop) % NZ, NZ - hop, dev(dz=1)
        else:
            src, dst, to = hop - 1, hop, dev(dz=NZ - 1)
        n = (k * 2 + way) * 4 + hop - 1
        return remote(
            rows.at[src * TOK : (src + 1) * TOK, lo:hi], rows.at[dst * TOK : (dst + 1) * TOK, lo:hi],
            rs.at[n], rr.at[n], to,
        )

    def ring(k, hop):
        if hop == 0:
            if k in own:
                own[k].wait()
            else:
                xcopy[k].wait_recv()
        for way in range(2):
            if 0 < hop <= HOPS[k][way]:
                ring_copy(k, way, hop).wait_recv()
            if hop < HOPS[k][way]:
                copy = ring_copy(k, way, hop + 1)
                copy.start()
                ring_copies.append(copy)

    gcopy = []

    def send_gates():
        for o in range(1, NX):
            mcopy[o].wait_recv()
        for d in range(1, NZ):
            copy = remote(meta.at[:, d], plane.at[:, NZ - d], gs.at[d], gr.at[d], dev(dz=d))
            copy.start()
            gcopy.append(copy)
        plane[:, 0] = meta[:, 0]

    def make_targets():
        for copy in gcopy:
            copy.wait_recv()
        a = lax.broadcasted_iota(I32, (TOK, TOK), 0)
        b = lax.broadcasted_iota(I32, (TOK, TOK), 1)
        earlier = jnp.where(a < b, 1.0, 0.0).astype(BF16)
        n = NZ * GROUPS
        base = CAP * (lax.broadcasted_iota(I32, (n, TOK), 0) // GROUPS)
        for o in range(NX):
            chosen = plane[o].reshape(n, TOK) != 0.0
            position = jnp.dot(jnp.where(chosen, 1.0, 0.0).astype(BF16), earlier, preferred_element_type=F32)
            target[o] = jnp.where(chosen, position.astype(I32) + base, -1).reshape(NZ, GROUPS, TOK)

    ycopies = {}

    def ycopy(k, j):
        lo, w = COL[k], CHUNKS[k][2]
        dc, dy = j // NY, lax.rem(j, NY)
        group = dc * NY + lax.rem(NY - dy, NY)
        n = k * GROUPS + j
        return remote(
            sendbuf.at[k % NSB, j, :, 0:w],
            routed.at[pl.ds(pl.multiple_of(group * PART, 16), PART), lo : lo + w],
            ys.at[n], yr.at[n], dev(dc=dc, dy=dy),
        )

    def select(k):
        o, _, w = CHUNKS[k]
        lo = COL[k]
        if k >= NSB:
            for j in range(1, GROUPS):
                ycopy(k - NSB, j).wait_send()
        slot = lax.broadcasted_iota(I32, (PART, TOK), 0)

        def picked(j):
            hits, gate = [], jnp.zeros((PART, TOK), F32)
            for d in range(NZ):
                hit = slot == target[o, d, pl.ds(j, 1), :]
                hits.append(jnp.where(hit, 1.0, 0.0).astype(BF16))
                gate += jnp.where(hit, plane[o, d, pl.ds(j, 1), :], 0.0)
            gate = jnp.sum(gate, axis=1, keepdims=True)
            chosen = jnp.dot(
                jnp.concatenate(hits, axis=1), rows[:, lo : lo + w], preferred_element_type=F32
            )
            return (chosen * gate).astype(BF16)

        def one(j, _):
            sendbuf[k % NSB, j, :, 0:w] = picked(j)
            ycopy(k, j).start()
            return 0

        lax.fori_loop(1, GROUPS, one, 0)
        routed[0:PART, lo : lo + w] = picked(0)

    def arrived(k):
        for j in range(1, GROUPS):
            ycopy(k, j).wait_recv()

    def hidden_product(k, fresh):
        _, first, w = CHUNKS[k]
        lo = COL[k]

        def one(t, _):
            at = pl.ds(pl.multiple_of(t * TILE, TILE), TILE)
            got = jnp.dot(routed[at, lo : lo + w], wts[first : first + w, :], preferred_element_type=F32)
            acc[at, :] = got if fresh else acc[at, :] + got
            return 0

        lax.fori_loop(0, SLOTS // TILE, one, 0)

    def weight_product(k, fresh):
        o, first, w = CHUNKS[k]
        lo = COL[k]

        def one(t, _):
            got = lax.dot_general(
                routed[:, pl.ds(pl.multiple_of(lo + t * TILE, TILE), TILE)], hid[o],
                (((0,), (0,)), ((), ())), preferred_element_type=F32,
            )
            at = pl.ds(pl.multiple_of(first + t * TILE, TILE), TILE)
            wg_out[0, at, :] = got if fresh else wg_out[0, at, :] + got
            return 0

        lax.fori_loop(0, w // TILE, one, 0)

    def origin(n):
        block = ((n.astype(F32) + 0.5) * (1.0 / CAP)).astype(I32)
        slot = n - block * CAP
        group = ((block.astype(F32) + 0.5) * (1.0 / NZ)).astype(I32)
        d = block - group * NZ
        dc = jnp.where(group >= NY, 1, 0)
        dy = group - dc * NY
        dz = z + d
        dz = jnp.where(dz >= NZ, dz - NZ, dz)
        dy = y + dy
        dy = jnp.where(dy >= NY, dy - NY, dy)
        dc = c + dc
        dc = jnp.where(dc >= NC, dc - NC, dc)
        return CAP * (dz * GROUPS + dc * NY + dy) + slot

    hcopy = {}

    def send_hidden():
        load_hidden.wait()

        def one(t, _):
            n = lax.broadcasted_iota(I32, (TILE, 1), 0) + t * TILE
            m = lax.broadcasted_iota(I32, (TILE, SLOTS), 1)
            pick = jnp.where(origin(n) == m, 1.0, 0.0).astype(BF16)
            at = pl.ds(pl.multiple_of(t * TILE, TILE), TILE)
            hid[0, at, :] = jnp.dot(pick, raw[...], preferred_element_type=F32).astype(BF16)
            return 0

        lax.fori_loop(0, SLOTS // TILE, one, 0)
        hcopy[0] = remote(hid.at[0], hid.at[3], hs.at[0], hr.at[0], dev(dx=1))
        hcopy[1] = remote(hid.at[0], hid.at[1], hs.at[1], hr.at[1], dev(dx=NX - 1))
        hcopy[0].start()
        hcopy[1].start()

    def pass_hidden():
        hcopy[0].wait_recv()
        hcopy[2] = remote(hid.at[3, 0:HALF], hid.at[2, 0:HALF], hs.at[2], hr.at[2], dev(dx=1))
        hcopy[2].start()
        hcopy[1].wait_recv()
        hcopy[3] = remote(hid.at[1, HALF:SLOTS], hid.at[2, HALF:SLOTS], hs.at[3], hr.at[3], dev(dx=NX - 1))
        hcopy[3].start()

    def got_far_hidden():
        hcopy[2].wait_recv()
        hcopy[3].wait_recv()

    pcopy = {}

    def send_far():
        part[1] = acc[...].astype(BF16)
        pcopy[0] = remote(part.at[1, 0:HALF], part2.at[0], ps.at[0], pr.at[0], dev(dx=1))
        pcopy[1] = remote(part.at[1, HALF:SLOTS], part2.at[1], ps.at[1], pr.at[1], dev(dx=NX - 1))
        pcopy[0].start()
        pcopy[1].start()

    def send_near(way):
        pcopy[way].wait_recv()
        if way == 0:
            part[0, 0:HALF] = (acc[0:HALF] + part2[0].astype(F32)).astype(BF16)
            part[0, HALF:SLOTS] = acc[HALF:SLOTS].astype(BF16)
            pcopy[2] = remote(part.at[0], partr.at[0], ps.at[2], pr.at[2], dev(dx=1))
            pcopy[2].start()
        else:
            part[2, 0:HALF] = acc[0:HALF].astype(BF16)
            part[2, HALF:SLOTS] = (acc[HALF:SLOTS] + part2[1].astype(F32)).astype(BF16)
            pcopy[3] = remote(part.at[2], partr.at[1], ps.at[3], pr.at[3], dev(dx=NX - 1))
            pcopy[3].start()

    def finish():
        pcopy[2].wait_recv()
        pcopy[3].wait_recv()
        total = acc[...] + partr[0].astype(F32) + partr[1].astype(F32)
        part[1] = total.astype(BF16)

        def one(t, _):
            n = lax.broadcasted_iota(I32, (1, SLOTS), 1)
            m = lax.broadcasted_iota(I32, (TILE, SLOTS), 0) + t * TILE
            pick = jnp.where(origin(n) == m, 1.0, 0.0).astype(BF16)
            at = pl.ds(pl.multiple_of(t * TILE, TILE), TILE)
            dh_out[0, 0, at, :] = jnp.dot(pick, part[1], preferred_element_type=F32).astype(BF16)
            return 0

        lax.fori_loop(0, SLOTS // TILE, one, 0)

    started = {}

    def weight_step(k):
        o, first, w = CHUNKS[k]
        fresh = first not in started
        started[first] = True
        weight_product(k, fresh)

    def main(k):
        arrived(k)
        if k == 0:
            wg_out[...] = jnp.zeros_like(wg_out)
            weight_product(0, False)
        elif k in (1, 2):
            if k == 1:
                load_weight.wait()
            hidden_product(k, k == 1)
            if k == 2:
                send_far()
        elif k in (3, 4):
            hidden_product(k, k == 3)
            if k == 4:
                send_near(0)
            weight_product(k, False)
        elif k in (5, 6):
            hidden_product(k, k == 5)
            if k == 6:
                send_near(1)
                pcopy[0].wait_send()
                pcopy[1].wait_send()
                weight_product(5, False)
                weight_product(6, False)
            else:
                got_far_hidden()
                weight_product(1, False)
                weight_product(2, False)
        else:
            if k == 7:
                hidden_product(0, True)
            hidden_product(k, False)
            weight_product(k, False)

    for q in range(2 * NK + 7):
        for k in range(NK):
            if 0 <= q - 2 * k <= 4:
                ring(k, q - 2 * k)
        if q == 0:
            send_gates()
        if q == 1:
            send_hidden()
        if q == 2:
            make_targets()
        k, odd = divmod(q - 4, 2)
        if 0 <= k < NK and not odd:
            select(k)
        k, odd = divmod(q - 7, 2)
        if 0 <= k < NK and not odd:
            main(k)
        if q == 8:
            pass_hidden()
    finish()

    for o in range(1, NX):
        mcopy[o].wait_send()
    for k in xcopy:
        xcopy[k].wait_send()
    for copy in gcopy + ring_copies:
        copy.wait_send()
    for k in range(max(0, NK - NSB), NK):
        for j in range(1, GROUPS):
            ycopy(k, j).wait_send()
    for n in range(4):
        hcopy[n].wait_send()
    pcopy[2].wait_send()
    pcopy[3].wait_send()


def body(d_out, route_ids, gate_weights, saved_hidden, down_weight):
    ids_t = route_ids[0].T
    gate_t = gate_weights[0].T
    vmem = pl.BlockSpec(memory_space=pltpu.VMEM)
    hbm = pl.BlockSpec(memory_space=pl.ANY)
    dma = pltpu.SemaphoreType.DMA
    return pl.pallas_call(
        kernel,
        out_shape=(
            jax.ShapeDtypeStruct((1, 1, SLOTS, FF), BF16),
            jax.ShapeDtypeStruct((1, WIDTH, FF), F32),
        ),
        in_specs=[hbm, vmem, vmem, hbm, hbm],
        out_specs=(vmem, vmem),
        scratch_shapes=[
            pltpu.VMEM((NZ * TOK, NX * WIDTH), BF16),
            pltpu.VMEM((NSB, GROUPS, PART, WMAX), BF16),
            pltpu.VMEM((SLOTS, NX * WIDTH), BF16),
            pltpu.VMEM((NX, SLOTS, FF), BF16),
            pltpu.VMEM((SLOTS, FF), BF16),
            pltpu.VMEM((WIDTH, FF), BF16),
            pltpu.VMEM((SLOTS, FF), F32),
            pltpu.VMEM((3, SLOTS, FF), BF16),
            pltpu.VMEM((2, HALF, FF), BF16),
            pltpu.VMEM((2, SLOTS, FF), BF16),
            pltpu.VMEM((NX, NZ, GROUPS, TOK), F32),
            pltpu.VMEM((NX, NZ, GROUPS, TOK), F32),
            pltpu.VMEM((NX, NZ, GROUPS, TOK), I32),
            dma((2 + NK,)),
            dma((NK,)), dma((NK,)),
            dma((NX,)), dma((NX,)),
            dma((NZ,)), dma((NZ,)),
            dma((NK * 8,)), dma((NK * 8,)),
            dma((NK * GROUPS,)), dma((NK * GROUPS,)),
            dma((4,)), dma((4,)),
            dma((4,)), dma((4,)),
        ],
        compiler_params=pltpu.CompilerParams(
            collective_id=0, has_side_effects=True, vmem_limit_bytes=62 * 2**20
        ),
        name="expert_backward",
    )(d_out, ids_t, gate_t, saved_hidden, down_weight)


def solution(mesh):
    return jax.shard_map(
        body,
        mesh=mesh,
        in_specs=(
            P("dp", ("ctx", "exp"), None),
            P("dp", ("ctx", "exp"), None),
            P("dp", ("ctx", "exp"), None),
            P("dp", ("ctx", "exp"), None, None),
            P(("ctx", "exp"), "dp", None),
        ),
        out_specs=(P("dp", ("ctx", "exp"), None, None), P(("ctx", "exp"), "dp", None)),
        check_vma=False,
    )
```

time: 504 us -> 193 us (0.38)
  waiting for transfers between devices: 356 us -> 0 us
  Pallas kernels: 0 us -> 182 us
  local copies, waits for them, and re-layouts: 76 us -> 9.35 us
  matrix products: 27.8 us -> 0 us
  between operations: 14.1 us -> 0.64 us
  other arithmetic: 13 us -> 0 us
  starting transfers between devices: 12.4 us -> 0 us
    all_to_all x1 -> x0, waiting for transfers between devices: 227 us -> none  [body(): lax.all_to_all(by_peer, ('ctx', 'exp'), split_axis=0, concat_axis=0, tile...]
    pallas_call x0 -> x1, Pallas kernels: none -> 182 us  [body(): pl.pallas_call(kernel, out_shape=(jax.ShapeDtypeStruct((1, 1, SLOTS, FF),...]
    reduce_scatter x1 -> x0, waiting for transfers between devices: 129 us -> none  [body(): lax.psum_scatter(lax.dot_general(columns, hidden, (((0,), (0,)), ((), ())...]
    dot_general x2 -> x0, matrix products: 27.8 us -> none  [the longest x1 14.8 us: body(): lax.dot_general(columns, hidden, (((0,), (0,)), ((), ())), preferred_elem...]
    reshape x2 -> x0, local copies, waits for them, and re-layouts: 27 us -> none  [the longest x1 13.6 us: body(): routed = arrived.reshape(expert_count * capacity, model_width)]
    mul x5 -> x0, local copies, waits for them, and re-layouts: 26.4 us -> none  [the longest x3 26.1 us: body(): gate_weights[0][:, :, None] * d_out[0][:, None, :].astype(jnp.float32)]
    scatter x1 -> x0, local copies, waits for them, and re-layouts: 21 us -> none  [body(): jnp.zeros((expert_count * capacity, model_width), jnp.bfloat16).at[target]]
    all_to_all x1 -> x0, starting transfers between devices: 12.3 us -> none  [body(): lax.all_to_all(by_peer, ('ctx', 'exp'), split_axis=0, concat_axis=0, tile...]
  transfers between devices with their start and end apart: 3 -> 0, of which waited for: 2 -> 0; matrix products, arithmetic and copies ran while one was open for 8% -> 0% of each run, Pallas kernels for 0% -> 0%
where the time goes in v1:
time: 193 us; the launch traced here: 192 us
  Pallas kernels  182 us (94%)
  local copies, waits for them, and re-layouts  9.35 us (5%)
    pallas_call x1, Pallas kernels, body(): pl.pallas_call(kernel, out_shape=(jax.ShapeDtypeStruct((1, 1, SLOTS, FF),...  182 us
    unnamed x4, local copies, waits for them, and re-layouts  9.35 us

profile of v1, /device:TPU:6, one launch (start us, length us, event | category | flops | bytes accessed | tf_op | source)
XLA Modules:
  0.0 192.5 jit_solution(1063919453086596998)
XLA Ops:
  0.6 1.3 copy.12
  1.9 1.3 copy.11
  3.2 182.5 %expert_backward.1 = (bf16[1,1,896,768]{3,2,1,0:T(8,128)(2,1)}, f32[1,1280,768]{2,1,0:T(8,128)}) custom-call(bf16[1,128,5120]{2,1,0:T(8,128)(2,1)} %d_out.1, s32[6,128]{1,0:T(8,128)} %bitcast.10, f32[6,128]{1,0:T(8,128)} %bitcast.11, bf16[1,1,896,768]{3,2,1,0:T(8,128)(2,1)} %hidden.1, bf16[1,1280,768]{2,1,0:T(8,128)(2,1)} %weight.1), custom_call_target="tpu_custom_call" | custom-call | tf_op jit(solution)/shard_map/expert_backward/pallas_call | solution.py:398
  185.7 2.5 %copy.15 = bf16[1,1,896,768]{3,2,1,0:T(8,128)(2,1)} copy(bf16[1,1,896,768]{3,2,1,0:T(8,128)(2,1)} %get-tuple-element.4) | data formatting | bytes 2752512
  188.2 4.3 %copy.16 = f32[1,1280,768]{2,1,0:T(8,128)} copy(f32[1,1280,768]{2,1,0:T(8,128)} %get-tuple-element.5) | data formatting | bytes 7864320

commit v2 on v1

--- a/solution.py
+++ b/solution.py
@@ -20,21 +20,25 @@
 TILE = 128
 
 CHUNKS = (
-    (0, 0, 256),
-    (2, 0, 640),
+    (2, 0, 256),
+    (2, 256, 384),
     (2, 640, 640),
     (1, 0, 640),
     (1, 640, 640),
     (3, 0, 640),
     (3, 640, 640),
-    (0, 256, 512),
-    (0, 768, 512),
+    (0, 0, 640),
+    (0, 640, 384),
+    (0, 1024, 256),
 )
 NK = len(CHUNKS)
 COL = [sum(c[2] for c in CHUNKS[:k]) for k in range(NK)]
 WMAX = max(c[2] for c in CHUNKS)
 NSB = 3
-HOPS = [(4, 3) if k % 2 == 0 else (3, 4) for k in range(NK)]
+LAST = NZ // 2
+MAIN_LAG = 7
+HIDDEN_AT, PASS_AT = 5, 10
+FEATURES_AT = {0: (1, 2), 2: (3,), 4: (4,), 6: (5, 6)}
 
 
 def kernel(
@@ -90,19 +94,22 @@
 
     pl.semaphore_wait(barrier, len(peers))
 
+    xcopy = {}
+
+    def send_features(k):
+        o, first, w = CHUNKS[k]
+        start = pl.multiple_of(lax.rem(i + NX - o, NX) * WIDTH + first, 128)
+        xcopy[k] = remote(
+            d_out.at[0, :, pl.ds(start, w)], rows.at[0:TOK, COL[k] : COL[k] + w],
+            xs.at[k], xr.at[k], dev(dx=NX - o),
+        )
+        xcopy[k].start()
+
+    send_features(0)
     mcopy = {}
     for o in range(1, NX):
         mcopy[o] = remote(meta.at[0], meta.at[o], ms.at[o], mr.at[o], dev(dx=NX - o))
         mcopy[o].start()
-    xcopy = {}
-    for k, (o, first, w) in enumerate(CHUNKS):
-        if o:
-            start = pl.multiple_of(lax.rem(i + NX - o, NX) * WIDTH + first, 128)
-            xcopy[k] = remote(
-                d_out.at[0, :, pl.ds(start, w)], rows.at[0:TOK, COL[k] : COL[k] + w],
-                xs.at[k], xr.at[k], dev(dx=NX - o),
-            )
-            xcopy[k].start()
 
     ring_copies = []
 
@@ -112,11 +119,12 @@
             src, dst, to = (NZ + 1 - hop) % NZ, NZ - hop, dev(dz=1)
         else:
             src, dst, to = hop - 1, hop, dev(dz=NZ - 1)
-        n = (k * 2 + way) * 4 + hop - 1
-        return remote(
-            rows.at[src * TOK : (src + 1) * TOK, lo:hi], rows.at[dst * TOK : (dst + 1) * TOK, lo:hi],
-            rs.at[n], rr.at[n], to,
-        )
+        first, n = 0, TOK
+        if hop == LAST:
+            first, n = way * (TOK // 2), TOK // 2
+        src, dst = src * TOK + first, dst * TOK + first
+        sem = (k * 2 + way) * LAST + hop - 1
+        return remote(rows.at[src : src + n, lo:hi], rows.at[dst : dst + n, lo:hi], rs.at[sem], rr.at[sem], to)
 
     def ring(k, hop):
         if hop == 0:
@@ -125,9 +133,9 @@
             else:
                 xcopy[k].wait_recv()
         for way in range(2):
-            if 0 < hop <= HOPS[k][way]:
+            if hop > 0:
                 ring_copy(k, way, hop).wait_recv()
-            if hop < HOPS[k][way]:
+            if hop < LAST:
                 copy = ring_copy(k, way, hop + 1)
                 copy.start()
                 ring_copies.append(copy)
@@ -213,7 +221,7 @@
 
         lax.fori_loop(0, SLOTS // TILE, one, 0)
 
-    def weight_product(k, fresh):
+    def weight_product(k):
         o, first, w = CHUNKS[k]
         lo = COL[k]
 
@@ -223,7 +231,7 @@
                 (((0,), (0,)), ((), ())), preferred_element_type=F32,
             )
             at = pl.ds(pl.multiple_of(first + t * TILE, TILE), TILE)
-            wg_out[0, at, :] = got if fresh else wg_out[0, at, :] + got
+            wg_out[0, at, :] += got
             return 0
 
         lax.fori_loop(0, w // TILE, one, 0)
@@ -312,66 +320,53 @@
 
         lax.fori_loop(0, SLOTS // TILE, one, 0)
 
-    started = {}
-
-    def weight_step(k):
+    for first in range(0, WIDTH, TILE):
+        wg_out[0, first : first + TILE, :] = jnp.zeros((TILE, FF), F32)
+
+    def main(k):
         o, first, w = CHUNKS[k]
-        fresh = first not in started
-        started[first] = True
-        weight_product(k, fresh)
-
-    def main(k):
         arrived(k)
         if k == 0:
-            wg_out[...] = jnp.zeros_like(wg_out)
-            weight_product(0, False)
-        elif k in (1, 2):
-            if k == 1:
-                load_weight.wait()
-            hidden_product(k, k == 1)
-            if k == 2:
+            load_weight.wait()
+        hidden_product(k, first == 0)
+        if first + w == WIDTH:
+            if o == 2:
                 send_far()
-        elif k in (3, 4):
-            hidden_product(k, k == 3)
-            if k == 4:
+            elif o == 1:
                 send_near(0)
-            weight_product(k, False)
-        elif k in (5, 6):
-            hidden_product(k, k == 5)
-            if k == 6:
+            elif o == 3:
                 send_near(1)
                 pcopy[0].wait_send()
                 pcopy[1].wait_send()
-                weight_product(5, False)
-                weight_product(6, False)
-            else:
-                got_far_hidden()
-                weight_product(1, False)
-                weight_product(2, False)
-        else:
-            if k == 7:
-                hidden_product(0, True)
-            hidden_product(k, False)
-            weight_product(k, False)
-
-    for q in range(2 * NK + 7):
-        for k in range(NK):
-            if 0 <= q - 2 * k <= 4:
+        if o != 2:
+            weight_product(k)
+        if (o, first) == (3, 0):
+            got_far_hidden()
+        if o == 3:
+            for m in range(NK):
+                if CHUNKS[m][0] == 2 and (CHUNKS[m][1] < WIDTH // 2) == (first == 0):
+                    weight_product(m)
+
+    for q in range(2 * NK + MAIN_LAG):
+        for k in reversed(range(NK)):
+            if 0 <= q - 2 * k <= LAST:
                 ring(k, q - 2 * k)
+        for k in FEATURES_AT.get(q, ()):
+            send_features(k)
         if q == 0:
             send_gates()
-        if q == 1:
-            send_hidden()
         if q == 2:
             make_targets()
-        k, odd = divmod(q - 4, 2)
+        if q == HIDDEN_AT:
+            send_hidden()
+        if q == PASS_AT:
+            pass_hidden()
+        k, odd = divmod(q - LAST, 2)
         if 0 <= k < NK and not odd:
             select(k)
-        k, odd = divmod(q - 7, 2)
+        k, odd = divmod(q - MAIN_LAG, 2)
         if 0 <= k < NK and not odd:
             main(k)
-        if q == 8:
-            pass_hidden()
     finish()
 
     for o in range(1, NX):

time: 193 us -> 178 us (0.922)
  Pallas kernels: 182 us -> 167 us
    pallas_call x1, Pallas kernels: 182 us -> 167 us  [body(): pl.pallas_call(kernel, out_shape=(jax.ShapeDtypeStruct((1, 1, SLOTS, FF),...]
where the time goes in v2:
time: 178 us; the launch traced here: 177 us
  Pallas kernels  167 us (94%)
  local copies, waits for them, and re-layouts  9.35 us (5%)
    pallas_call x1, Pallas kernels, body(): pl.pallas_call(kernel, out_shape=(jax.ShapeDtypeStruct((1, 1, SLOTS, FF),...  167 us
    unnamed x4, local copies, waits for them, and re-layouts  9.35 us

profile of v2, /device:TPU:6, one launch (start us, length us, event | category | flops | bytes accessed | tf_op | source)
XLA Modules:
  0.0 177.4 jit_solution(4013681283265957908)
XLA Ops:
  0.6 1.3 copy.12
  1.9 1.3 copy.11
  3.2 167.4 %expert_backward.1 = (bf16[1,1,896,768]{3,2,1,0:T(8,128)(2,1)}, f32[1,1280,768]{2,1,0:T(8,128)}) custom-call(bf16[1,128,5120]{2,1,0:T(8,128)(2,1)} %d_out.1, s32[6,128]{1,0:T(8,128)} %bitcast.10, f32[6,128]{1,0:T(8,128)} %bitcast.11, bf16[1,1,896,768]{3,2,1,0:T(8,128)(2,1)} %hidden.1, bf16[1,1280,768]{2,1,0:T(8,128)(2,1)} %weight.1), custom_call_target="tpu_custom_call" | custom-call | tf_op jit(solution)/shard_map/expert_backward/pallas_call | solution.py:393
  170.6 2.5 %copy.15 = bf16[1,1,896,768]{3,2,1,0:T(8,128)(2,1)} copy(bf16[1,1,896,768]{3,2,1,0:T(8,128)(2,1)} %get-tuple-element.4) | data formatting | bytes 2752512
  173.1 4.3 %copy.16 = f32[1,1280,768]{2,1,0:T(8,128)} copy(f32[1,1280,768]{2,1,0:T(8,128)} %get-tuple-element.5) | data formatting | bytes 7864320

commit v3 on v2

--- a/solution.py
+++ b/solution.py
@@ -37,8 +37,8 @@
 NSB = 3
 LAST = NZ // 2
 MAIN_LAG = 7
-HIDDEN_AT, PASS_AT = 5, 10
-FEATURES_AT = {0: (1, 2), 2: (3,), 4: (4,), 6: (5, 6)}
+HIDDEN_AT, PASS_AT = 4, 9
+FEATURES_AT = {0: (1, 2), 2: (3, 4), 3: (5, 6)}
 
 
 def kernel(
@@ -319,9 +319,6 @@
             return 0
 
         lax.fori_loop(0, SLOTS // TILE, one, 0)
-
-    for first in range(0, WIDTH, TILE):
-        wg_out[0, first : first + TILE, :] = jnp.zeros((TILE, FF), F32)
 
     def main(k):
         o, first, w = CHUNKS[k]
@@ -355,6 +352,9 @@
             send_features(k)
         if q == 0:
             send_gates()
+        if q == 1:
+            for first in range(0, WIDTH, TILE):
+                wg_out[0, first : first + TILE, :] = jnp.zeros((TILE, FF), F32)
         if q == 2:
             make_targets()
         if q == HIDDEN_AT:

time: 178 us -> 171 us (0.961)
  Pallas kernels: 167 us -> 161 us
    pallas_call x1, Pallas kernels: 167 us -> 161 us  [body(): pl.pallas_call(kernel, out_shape=(jax.ShapeDtypeStruct((1, 1, SLOTS, FF),...]
where the time goes in v3:
time: 171 us; the launch traced here: 170 us
  Pallas kernels  161 us (94%)
  local copies, waits for them, and re-layouts  9.35 us (5%)
    pallas_call x1, Pallas kernels, body(): pl.pallas_call(kernel, out_shape=(jax.ShapeDtypeStruct((1, 1, SLOTS, FF),...  161 us
    unnamed x4, local copies, waits for them, and re-layouts  9.35 us

profile of v3, /device:TPU:6, one launch (start us, length us, event | category | flops | bytes accessed | tf_op | source)
XLA Modules:
  0.0 170.5 jit_solution(13728428888823895279)
XLA Ops:
  0.6 1.3 copy.12
  1.9 1.3 copy.11
  3.2 160.5 %expert_backward.1 = (bf16[1,1,896,768]{3,2,1,0:T(8,128)(2,1)}, f32[1,1280,768]{2,1,0:T(8,128)}) custom-call(bf16[1,128,5120]{2,1,0:T(8,128)(2,1)} %d_out.1, s32[6,128]{1,0:T(8,128)} %bitcast.10, f32[6,128]{1,0:T(8,128)} %bitcast.11, bf16[1,1,896,768]{3,2,1,0:T(8,128)(2,1)} %hidden.1, bf16[1,1280,768]{2,1,0:T(8,128)(2,1)} %weight.1), custom_call_target="tpu_custom_call" | custom-call | tf_op jit(solution)/shard_map/expert_backward/pallas_call | solution.py:393
  163.7 2.5 %copy.15 = bf16[1,1,896,768]{3,2,1,0:T(8,128)(2,1)} copy(bf16[1,1,896,768]{3,2,1,0:T(8,128)(2,1)} %get-tuple-element.4) | data formatting | bytes 2752512
  166.2 4.3 %copy.16 = f32[1,1280,768]{2,1,0:T(8,128)} copy(f32[1,1280,768]{2,1,0:T(8,128)} %get-tuple-element.5) | data formatting | bytes 7864320

commit v4 on v3

--- a/solution.py
+++ b/solution.py
@@ -37,8 +37,8 @@
 NSB = 3
 LAST = NZ // 2
 MAIN_LAG = 7
-HIDDEN_AT, PASS_AT = 4, 9
-FEATURES_AT = {0: (1, 2), 2: (3, 4), 3: (5, 6)}
+HIDDEN_AT, PASS_AT = 3, 8
+FEATURES_AT = {0: (1, 2), 1: (3, 4), 2: (5, 6)}
 
 
 def kernel(

time: 171 us -> 180 us (1.053); the launches traced: 170 us -> 177 us
  Pallas kernels: 161 us -> 167 us
    pallas_call x1, Pallas kernels: 161 us -> 167 us  [body(): pl.pallas_call(kernel, out_shape=(jax.ShapeDtypeStruct((1, 1, SLOTS, FF),...]
where the time goes in v4:
time: 180 us; the launch traced here: 177 us
  Pallas kernels  167 us (93%)
  local copies, waits for them, and re-layouts  9.35 us (5%)
    pallas_call x1, Pallas kernels, body(): pl.pallas_call(kernel, out_shape=(jax.ShapeDtypeStruct((1, 1, SLOTS, FF),...  167 us
    unnamed x4, local copies, waits for them, and re-layouts  9.35 us

profile of v4, /device:TPU:6, one launch (start us, length us, event | category | flops | bytes accessed | tf_op | source)
XLA Modules:
  0.0 177.5 jit_solution(6918543963273251364)
XLA Ops:
  0.6 1.3 copy.12
  1.9 1.3 copy.11
  3.2 167.5 %expert_backward.1 = (bf16[1,1,896,768]{3,2,1,0:T(8,128)(2,1)}, f32[1,1280,768]{2,1,0:T(8,128)}) custom-call(bf16[1,128,5120]{2,1,0:T(8,128)(2,1)} %d_out.1, s32[6,128]{1,0:T(8,128)} %bitcast.10, f32[6,128]{1,0:T(8,128)} %bitcast.11, bf16[1,1,896,768]{3,2,1,0:T(8,128)(2,1)} %hidden.1, bf16[1,1280,768]{2,1,0:T(8,128)(2,1)} %weight.1), custom_call_target="tpu_custom_call" | custom-call | tf_op jit(solution)/shard_map/expert_backward/pallas_call | solution.py:393
  170.7 2.5 %copy.15 = bf16[1,1,896,768]{3,2,1,0:T(8,128)(2,1)} copy(bf16[1,1,896,768]{3,2,1,0:T(8,128)(2,1)} %get-tuple-element.4) | data formatting | bytes 2752512
  173.2 4.3 %copy.16 = f32[1,1280,768]{2,1,0:T(8,128)} copy(f32[1,1280,768]{2,1,0:T(8,128)} %get-tuple-element.5) | data formatting | bytes 7864320
